TPU v7x, 128 devices: a whole 4x4x4 slice. The times are simulated.
128 devices in a mesh: pos: 32 (over z, y, x_hi), depth: 2 (over x_lo), det: 2 (over core).
Axes of the slice: x: 4 (x_hi: 2, x_lo: 2; x = x_hi * 2 + x_lo), y: 4, z: 4, core: 2. Of those that a mesh axis runs over, the one named last changes fastest.
Arguments:
- offsets: int32 [256, 2], P('pos'), may hold values from 0 to 768
- counts: int32 [32], P('pos'), may hold values from 1 to 8, 128 in all
- probe_wave: bfloat16 [2, 256, 256], P(None, 'det'), may hold values from -4.1875 to 4.1875
- object_slices: float32 [2, 2, 1024, 1024], P('depth'), may hold values from -1.35 to 1.35, as said below
- measured: float32 [256, 256, 256], P('pos', 'det'), may hold values from 0 to 2
Outputs:
- slice_gradient: float32 [2, 2, 1024, 1024], P('depth', None, ('pos', 'det'))
Inputs may be any that keep to these rules, and one draw needn't show every extreme that they name: The counts sum to 128; the largest is 8. `object_slices`: each (real, imaginary) pair is a transmission of modulus 0.74 to 1.35.
All inputs are finite; a program needn't handle non-finite values. No bound on the sum of `counts` on one device may be relied on, other than what follows from the above.
Results may differ from a plain program's by a relative error of at most 0.023.
Values may be sent and summed in bfloat16 or wider, within the bound.
A program may use at most 128 MiB of HBM per device.

v0:
```python
import math

import jax
import jax.numpy as jnp
import numpy as np
from jax import lax
from jax.experimental import pallas as pl
from jax.experimental.pallas import tpu as pltpu
from jax.sharding import PartitionSpec as P

PROP_DIV = 2
WIN = 256
HALF = WIN // 2
BANDS = 4
PLANE = 8
CAP = 8
CLS = 16
ROUTE = ((1, 0), (3, 0), (0, 1), (2, 0), (1, 1), (3, 1), (2, 1), (0, 0))
MESH = pl.DeviceIdType.MESH
BF = jnp.bfloat16
F32 = jnp.float32


def tables():
    k = np.arange(WIN)
    angle = (k[:, None] * k[None, :] % WIN) * (2.0 * math.pi / WIN)
    cos, sin = np.cos(angle), np.sin(angle)
    f = np.where(k < WIN // 2, k, k - WIN)
    h = np.exp(-1j * math.pi / (PROP_DIV * WIN) * (f * f % (2 * PROP_DIV * WIN)))
    dft = cos - 1j * sin
    q = (np.conj(dft) * h[None, :]) @ dft / WIN
    qr, qi = q.real, q.imag
    out = np.stack(
        [
            np.block([[cos, -sin], [sin, cos]]) / 16,
            np.block([[cos, sin], [-sin, cos]]) / 16,
            np.block([[qr, qi], [-qi, qr]]),
            np.block([[qr, -qi], [qi, qr]]),
        ]
    )
    return out.astype(np.float32).astype(BF)


def dot(a, b):
    return jnp.dot(a, b, preferred_element_type=F32)


def beside(re, im):
    return jnp.concatenate([re.astype(BF), im.astype(BF)], axis=1)


def stacked(re, im):
    return jnp.concatenate([re.astype(BF), im.astype(BF)], axis=0)


def right_left(re, im, right, left):
    mid = dot(beside(re, im), right).astype(BF)
    out = dot(left, jnp.concatenate([mid[:, :WIN], mid[:, WIN:]], axis=0))
    return out[:WIN], out[WIN:]


def left_right(re, im, left, right):
    mid = dot(left, stacked(re, im)).astype(BF)
    out = dot(jnp.concatenate([mid[:WIN], mid[WIN:]], axis=1), right)
    return out[:, :WIN], out[:, WIN:]


def iota(shape, axis):
    return lax.broadcasted_iota(jnp.int32, shape, axis)


def kernel(
    counts, offs_in, probe, obj, measured, tabs_in, out,
    offs, other_offs, obj_v, tabs, t_all, t_send, probe_v, meas, rolled, amps, grad, pieces, places, acc, z_send, z_recv,
    load_sem, own_sem, probe_sem, meas_sem, t_sem, t_out_sem, out_sem, place_sem, place_out_sem,
    piece_sem, piece_out_sem, z_sem, z_out_sem,
):
    pos, d, c = lax.axis_index("pos"), lax.axis_index("depth"), lax.axis_index("det")
    z, q = pos // PLANE, pos % PLANE
    y, x = q // 2, q % 2 * 2 + d
    cls = q * 2 + c
    other = z * PLANE + (q ^ 1)
    own = 2 * (2 * d + c)
    across = 2 * (2 * (1 - d) + c)
    beside_slot = 2 * (2 * d + 1 - c)

    own_offs = pltpu.make_async_copy(offs_in, offs, own_sem.at[3])
    own_offs.start()
    load_obj = []
    for cb in range(BANDS):
        column = obj.at[:, :, :, pl.ds(cb * WIN, WIN)]
        load_obj.append(pltpu.make_async_copy(column, obj_v.at[cb], load_sem.at[cb]))
        load_obj[-1].start()
    load_tabs = pltpu.make_async_copy(tabs_in, tabs, load_sem.at[BANDS])
    load_tabs.start()
    own_probe = pltpu.make_async_copy(probe, probe_v.at[c], own_sem.at[0])
    own_probe.start()
    own_meas = pltpu.make_async_copy(measured.at[pl.ds(own, 2)], meas.at[c], own_sem.at[1])
    own_meas.start()

    barrier = pltpu.get_barrier_semaphore()
    for k in range(1, 2 * CLS):
        pl.semaphore_signal(
            barrier, inc=1,
            device_id=(z * PLANE + (q ^ (k // 4)), d ^ (k // 2 % 2), c ^ (k % 2)),
            device_id_type=MESH,
        )
    for k in range(1, BANDS):
        pl.semaphore_signal(
            barrier, inc=1, device_id=((z + k) % BANDS * PLANE + q, d, c), device_id_type=MESH
        )

    own_offs.wait()
    slot_of = iota((CAP, 128), 0)
    for axis in range(2):
        spread = jnp.zeros((CAP, 128), jnp.int32)
        for s in range(CAP):
            spread = jnp.where(slot_of == s, offs[axis, s], spread)
        places[q, axis] = spread
    acc[...] = jnp.zeros_like(acc)
    pl.semaphore_wait(barrier, 2 * CLS - 1 + BANDS - 1)

    def place_copy(k):
        return pltpu.make_async_remote_copy(
            src_ref=places.at[q], dst_ref=places.at[q], send_sem=place_out_sem.at[k],
            recv_sem=place_sem.at[q], device_id=(z * PLANE + (q ^ k), d, c),
            device_id_type=MESH,
        )

    def places_of(g):
        return pltpu.make_async_copy(places.at[g], places.at[g], place_sem.at[g])

    place_copy(1).start()

    probe_copy = pltpu.make_async_remote_copy(
        src_ref=probe, dst_ref=probe_v.at[c], send_sem=out_sem.at[0], recv_sem=probe_sem,
        device_id=(pos, d, 1 - c), device_id_type=MESH,
    )
    probe_copy.start()
    meas_copy = pltpu.make_async_remote_copy(
        src_ref=measured.at[pl.ds(beside_slot, 2)], dst_ref=meas.at[c], send_sem=out_sem.at[1],
        recv_sem=meas_sem, device_id=(pos, d, 1 - c), device_id_type=MESH,
    )
    meas_copy.start()

    for column in load_obj:
        column.wait()

    row_of, col_of = iota((WIN, WIN), 0), iota((WIN, WIN), 1)

    half_row = iota((HALF, WIN), 0)
    half_col = iota((HALF, WIN), 1)

    def cut(r, col, half, plane):
        rows = pl.ds(half * HALF, HALF)
        band = jnp.minimum(r >> 8, BANDS - 2)
        block = jnp.minimum(col >> 8, BANDS - 2)
        late = half_col >= col - block * WIN
        top = jnp.where(
            late, obj_v[block, plane, band, rows], obj_v[block + 1, plane, band, rows]
        )
        low = jnp.where(
            late, obj_v[block, plane, band + 1, rows], obj_v[block + 1, plane, band + 1, rows]
        )
        return jnp.where(half_row >= r - band * WIN - half * HALF, top, low).astype(BF)

    def t_copy(i, half):
        there = pos + half * (other - pos)
        return pltpu.make_async_remote_copy(
            src_ref=t_send.at[i, half], dst_ref=t_all.at[d, i, half],
            send_sem=t_out_sem.at[i, half], recv_sem=t_sem.at[i, half],
            device_id=(there, 1 - d, c), device_id_type=MESH,
        )

    places_of(q ^ 1).wait()
    fetch = pltpu.make_async_copy(places.at[q ^ 1], other_offs, own_sem.at[2])
    fetch.start()
    fetch.wait()

    def send_half(n, carry):
        i, half = n // 2, (n + c) % 2
        r = jnp.where(half == 1, other_offs[0, across + i, 0], offs[0, across + i])
        col = jnp.where(half == 1, other_offs[1, across + i, 0], offs[1, across + i])
        for plane in range(2):
            t_send[i, half, plane] = cut(r, col, half, plane)
        t_copy(i, half).start()
        return carry

    def cut_own(i):
        for half in range(2):
            for plane in range(2):
                t_all[d, i, half, plane] = cut(
                    offs[0, own + i], offs[1, own + i], half, plane
                )

    lax.fori_loop(0, 2, send_half, 0)

    def window(s, i):
        return [
            jnp.concatenate([t_all[s, i, 0, p], t_all[s, i, 1, p]], axis=0).astype(F32)
            for p in range(2)
        ]

    def prepare(i):
        cut_own(i)
        flat = jnp.concatenate(
            [jnp.concatenate([probe_v[0, p], probe_v[1, p]], axis=0) for p in range(2)], axis=1
        )
        r, col = offs[0, own + i], offs[1, own + i]
        down = jnp.where(col_of == ((row_of - r) & (WIN - 1)), 1.0, 0.0).astype(BF)
        over = jnp.where(row_of == ((col_of - col) & (WIN - 1)), 1.0, 0.0).astype(BF)
        moved = dot(down, flat).astype(BF)
        moved = dot(jnp.concatenate([moved[:, :WIN], moved[:, WIN:]], axis=0), over)
        rolled[i, 0], rolled[i, 1] = moved[:WIN].astype(BF), moved[WIN:].astype(BF)
        amps[i] = jnp.concatenate([meas[0, i], meas[1, i]], axis=0).T

    own_probe.wait()
    own_meas.wait()
    probe_copy.wait_recv()
    meas_copy.wait_recv()
    prepare(0)
    lax.fori_loop(2, 4, send_half, 0)
    prepare(1)
    for k in range(2, PLANE):
        place_copy(k).start()
    load_tabs.wait()

    def send_pieces(i, s):
        odd = (s + d) % 2
        for dy, far in ROUTE:
            yy = (y + dy * (1 + 2 * c)) % 4
            xx = (x + odd + 2 * ((far + c * odd) % 2)) % 4
            for cc in range(2):
                if (dy, far, cc) == (0, 0, 0):
                    continue
                core = c ^ cc
                pltpu.make_async_remote_copy(
                    src_ref=grad.at[i, s, (yy * 2 + xx // 2) * 2 + core],
                    dst_ref=pieces.at[i, q, 2 * d + c],
                    send_sem=piece_out_sem.at[i, s], recv_sem=piece_sem.at[i, q],
                    device_id=(z * PLANE + yy * 2 + xx // 2, s, core), device_id_type=MESH,
                ).start()

    def send_here(i):
        xx = (x + 1 + 2 * c) % 4
        pltpu.make_async_remote_copy(
            src_ref=grad.at[i, 1 - d, (y * 2 + xx // 2) * 2 + c],
            dst_ref=pieces.at[i, q, 2 * d + c],
            send_sem=piece_out_sem.at[i, 0], recv_sem=piece_sem.at[i, q],
            device_id=(z * PLANE + y * 2 + xx // 2, 1 - d, c), device_id_type=MESH,
        ).start()
        pltpu.make_async_copy(
            grad.at[i, d, cls], pieces.at[i, q, 2 * d + c], piece_sem.at[i, q]
        ).start()

    def load(ref, i):
        return ref[i, 0].astype(F32), ref[i, 1].astype(F32)

    def rounded(pair):
        return pair[0].astype(BF).astype(F32), pair[1].astype(BF).astype(F32)

    def await_windows(i):
        for half in range(2):
            t_copy(i, half).wait_recv()

    def first_wave(i):
        pl.when(d == 1)(lambda: await_windows(i))
        (pr, pi), (tr, ti) = load(rolled, i), window(0, i)
        return rounded(
            right_left(pr * tr - pi * ti, pr * ti + pi * tr, tabs[2], tabs[3])
        )

    def far_field(i, wave):
        pl.when(d == 0)(lambda: await_windows(i))
        (wr, wi), (tr, ti) = wave, window(1, i)
        fr, fi = right_left(wr * tr - wi * ti, wr * ti + wi * tr, tabs[0], tabs[1])
        used = jnp.where(jnp.full((1, WIN), own + i, jnp.int32) < counts[0], 1.0, 0.0)
        scale = used * (1.0 - amps[i] * lax.rsqrt(jnp.maximum(fr * fr + fi * fi, 1.0)))
        return fr * scale, fi * scale

    def descent(residual):
        return rounded(left_right(residual[0], residual[1], tabs[0], tabs[1]))

    def put(i, s, wave, desc):
        (wr, wi), (dr, di) = wave, desc
        grad[i, s, :, 0] = (wr * dr + wi * di).astype(BF).reshape(CLS, 16, WIN)
        grad[i, s, :, 1] = (wr * di - wi * dr).astype(BF).reshape(CLS, 16, WIN)

    def first_descent(i, desc):
        (dr, di), (tr, ti) = desc, window(1, i)
        return rounded(
            right_left(tr * dr + ti * di, tr * di - ti * dr, tabs[3], tabs[2])
        )

    wave_a = first_wave(0)
    desc_a = descent(far_field(0, wave_a))
    put(0, 1, wave_a, desc_a)
    send_pieces(0, 1)
    wave_b = first_wave(1)
    desc_a = first_descent(0, desc_a)
    put(0, 0, load(rolled, 0), desc_a)
    send_pieces(0, 0)
    send_here(0)
    desc_b = descent(far_field(1, wave_b))
    put(1, 1, wave_b, desc_b)
    send_pieces(1, 1)
    put(1, 0, load(rolled, 1), first_descent(1, desc_b))
    send_pieces(1, 0)
    send_here(1)

    row16 = iota((2, 8, WIN), 0) * 8 + iota((2, 8, WIN), 1) + cls * 16
    col8 = iota((8, WIN), 1)

    def add_group(i, g):
        pltpu.make_async_copy(pieces.at[i, g], pieces.at[i, g], piece_sem.at[i, g]).wait()
        rows, cols = places[g, 0], places[g, 1]
        r0 = jnp.minimum(rows >> 8, BANDS - 2)
        c0 = jnp.minimum(cols >> 8, BANDS - 2)
        rm, cm = rows - r0 * WIN, cols - c0 * WIN

        def wide(x, k):
            one = jnp.broadcast_to(x[2 * k + i : 2 * k + i + 1], (8, 128))
            return jnp.concatenate([one, one], axis=1)

        band = [wide(r0, k) + jnp.where(row16 < wide(rm, k), 1, 0) for k in range(4)]
        block = [wide(c0, k) + jnp.where(col8 < wide(cm, k), 1, 0) for k in range(4)]
        for p in range(2):
            piece = [pieces[i, g, k, p].astype(F32).reshape(2, 8, WIN) for k in range(4)]
            for zb in range(BANDS):
                part = [jnp.where(b == zb, x, 0.0) for b, x in zip(band, piece)]
                for cb in range(BANDS):
                    total = acc[zb, p, :, :, cb * WIN : (cb + 1) * WIN]
                    for b, x in zip(block, part):
                        total += jnp.where(b == cb, x, 0.0)
                    acc[zb, p, :, :, cb * WIN : (cb + 1) * WIN] = total

    def add_first(k, carry):
        g = q ^ k ^ (k // 4 * 2)

        @pl.when(k > 1)
        def _():
            places_of(g).wait()

        add_group(0, g)
        return carry

    def add_second(k, carry):
        add_group(1, q ^ k ^ (k // 4 * 2))
        return carry

    lax.fori_loop(0, PLANE, add_first, 0)
    lax.fori_loop(0, PLANE, add_second, 0)

    z_send[...] = acc[...].reshape(BANDS, 2, 16, 1024).astype(BF)

    def z_copy(k):
        there = (z + k) % BANDS
        return pltpu.make_async_remote_copy(
            src_ref=z_send.at[there], dst_ref=z_recv.at[k], send_sem=z_out_sem.at[k],
            recv_sem=z_sem.at[k], device_id=(there * PLANE + q, d, c), device_id_type=MESH,
        )

    for k in (1 + 2 * c, 3 - 2 * c, 2):
        z_copy(k).start()
    total = acc[z].reshape(2, 16, 1024)
    for k in (1, 3, 2):
        z_copy(k).wait_recv()
        total += z_recv[k].astype(F32)
    out[...] = total

    for k in range(1, BANDS):
        z_copy(k).wait_send()
    probe_copy.wait_send()
    meas_copy.wait_send()
    for i in range(2):
        for half in range(2):
            t_copy(i, half).wait_send()
    for k in range(1, PLANE):
        place_copy(k).wait_send()
    for i in range(2):
        for s, count in ((0, CLS), (1, CLS - 1)):
            sent = grad.at[i, s, pl.ds(0, count)]
            pltpu.make_async_copy(sent, sent, piece_out_sem.at[i, s]).wait()


def per_device(offsets, counts, probe_wave, object_slices, measured):
    smem = pl.BlockSpec(memory_space=pltpu.SMEM)
    anywhere = pl.BlockSpec(memory_space=pl.ANY)
    dma = pltpu.SemaphoreType.DMA
    planes = object_slices.reshape(2, BANDS, WIN, BANDS * WIN)
    operands = (offsets.T, probe_wave, planes, measured, jnp.asarray(tables()))
    grad = pl.pallas_call(
        kernel,
        out_shape=pltpu.VMEM((2, 16, 1024), F32),
        in_specs=[smem] + [anywhere] * 5,
        out_specs=pl.BlockSpec(memory_space=pltpu.VMEM),
        scratch_shapes=[
            pltpu.SMEM((2, CAP), jnp.int32),
            pltpu.SMEM((2, CAP, 128), jnp.int32),
            pltpu.VMEM((BANDS, 2, BANDS, WIN, WIN), F32),
            pltpu.VMEM((4, 2 * WIN, 2 * WIN), BF),
            pltpu.VMEM((2, 2, 2, 2, HALF, WIN), BF),
            pltpu.VMEM((2, 2, 2, HALF, WIN), BF),
            pltpu.VMEM((2, 2, WIN // 2, WIN), BF),
            pltpu.VMEM((2, 2, WIN // 2, WIN), F32),
            pltpu.VMEM((2, 2, WIN, WIN), BF),
            pltpu.VMEM((2, WIN, WIN), F32),
            pltpu.VMEM((2, 2, CLS, 2, 16, WIN), BF),
            pltpu.VMEM((2, PLANE, CAP // 2, 2, 16, WIN), BF),
            pltpu.VMEM((PLANE, 2, CAP, 128), jnp.int32),
            pltpu.VMEM((BANDS, 2, 2, 8, 1024), F32),
            pltpu.VMEM((BANDS, 2, 16, 1024), BF),
            pltpu.VMEM((BANDS, 2, 16, 1024), BF),
            dma((BANDS + 1,)),
            dma((4,)),
            dma,
            dma,
            dma((2, 2)),
            dma((2, 2)),
            dma((2,)),
            dma((PLANE,)),
            dma((PLANE,)),
            dma((2, PLANE)),
            dma((2, 2)),
            dma((BANDS,)),
            dma((BANDS,)),
        ],
        compiler_params=pltpu.CompilerParams(
            collective_id=0, has_side_effects=True, vmem_limit_bytes=40 * 2**20
        ),
        cost_estimate=pl.CostEstimate(
            flops=2 * 16 * 2**27, bytes_accessed=12 * 2**20, transcendentals=0
        ),
    )(counts, *(pltpu.with_memory_space_constraint(a, pltpu.HBM) for a in operands))
    return grad[None]


def solution(mesh):
    in_specs = (
        P("pos", None),
        P("pos"),
        P(None, "det", None),
        P("depth", None, None, None),
        P("pos", "det", None),
    )
    out_specs = P("depth", None, ("pos", "det"), None)
    return jax.shard_map(
        per_device, mesh=mesh, in_specs=in_specs, out_specs=out_specs, check_vma=False
    )
```

profile of v0, /device:TPU:0, one launch (start us, length us, event | category | flops | bytes accessed | tf_op | source)
XLA Modules:
  0.0 41.6 jit_solution(9944964968523747060)
XLA Ops:
  0.7 40.3 %shard_map.64 = f32[2,16,1024]{2,1,0:T(8,128)S(1)} custom-call(s32[1]{0:T(128)S(6)} %copy.9.counts, s32[2,8]{1,0:T(2,128)} %bitcast.5, bf16[2,128,256]{2,1,0:T(8,128)(2,1)} %probe.1, f32[2,4,256,1024]{3,2,1,0:T(8,128)} %bitcast.4, f32[8,128,256]{2,1,0:T(8,128)} %measured.1, bf16[4,512,512]{2,1,0:T(8,128)(2,1)} %constant.2.clone.tabs_in), custom_call_target="tpu_custom_call" | custom-call | flops 4294967296 | bytes 12582912 | tf_op jit(solution)/shard_map/pallas_call | solution.py:392
  40.9 0.7 %copy.8 = f32[1,2,16,1024]{3,2,1,0:T(8,128)} copy(f32[1,2,16,1024]{3,2,1,0:T(8,128)S(1)} %bitcast.3) | data formatting | bytes 262144
where the time goes:
time: 41.7 us; the launch traced here: 41.6 us
  Pallas kernels  40.3 us (97%)
  local copies, waits for them, and re-layouts  0.66 us (2%)
  between operations  0.66 us (2%)
    pallas_call x1, Pallas kernels, per_device(): pl.pallas_call(kernel, out_shape=pltpu.VMEM((2, 16, 1024), F32), in_specs...  40.3 us

commit v1 on v0

--- a/solution.py
+++ b/solution.py
@@ -15,7 +15,7 @@
 PLANE = 8
 CAP = 8
 CLS = 16
-ROUTE = ((1, 0), (3, 0), (0, 1), (2, 0), (1, 1), (3, 1), (2, 1), (0, 0))
+ROUTE = ((2, 1), (2, 0), (0, 1), (1, 1), (3, 1), (1, 0), (3, 0), (0, 0))
 MESH = pl.DeviceIdType.MESH
 BF = jnp.bfloat16
 F32 = jnp.float32
@@ -186,14 +186,19 @@
         t_copy(i, half).start()
         return carry
 
-    def cut_own(i):
+    lax.fori_loop(0, 4, send_half, 0)
+    for k in range(2, PLANE):
+        place_copy(k).start()
+
+    def cut_own(i, carry):
         for half in range(2):
             for plane in range(2):
                 t_all[d, i, half, plane] = cut(
                     offs[0, own + i], offs[1, own + i], half, plane
                 )
-
-    lax.fori_loop(0, 2, send_half, 0)
+        return carry
+
+    lax.fori_loop(0, 2, cut_own, 0)
 
     def window(s, i):
         return [
@@ -201,11 +206,15 @@
             for p in range(2)
         ]
 
-    def prepare(i):
-        cut_own(i)
-        flat = jnp.concatenate(
-            [jnp.concatenate([probe_v[0, p], probe_v[1, p]], axis=0) for p in range(2)], axis=1
-        )
+    own_probe.wait()
+    own_meas.wait()
+    probe_copy.wait_recv()
+    meas_copy.wait_recv()
+
+    flat = jnp.concatenate(
+        [jnp.concatenate([probe_v[0, p], probe_v[1, p]], axis=0) for p in range(2)], axis=1
+    )
+    for i in range(2):
         r, col = offs[0, own + i], offs[1, own + i]
         down = jnp.where(col_of == ((row_of - r) & (WIN - 1)), 1.0, 0.0).astype(BF)
         over = jnp.where(row_of == ((col_of - col) & (WIN - 1)), 1.0, 0.0).astype(BF)
@@ -213,16 +222,6 @@
         moved = dot(jnp.concatenate([moved[:, :WIN], moved[:, WIN:]], axis=0), over)
         rolled[i, 0], rolled[i, 1] = moved[:WIN].astype(BF), moved[WIN:].astype(BF)
         amps[i] = jnp.concatenate([meas[0, i], meas[1, i]], axis=0).T
-
-    own_probe.wait()
-    own_meas.wait()
-    probe_copy.wait_recv()
-    meas_copy.wait_recv()
-    prepare(0)
-    lax.fori_loop(2, 4, send_half, 0)
-    prepare(1)
-    for k in range(2, PLANE):
-        place_copy(k).start()
     load_tabs.wait()
 
     def send_pieces(i, s):
@@ -259,19 +258,15 @@
     def rounded(pair):
         return pair[0].astype(BF).astype(F32), pair[1].astype(BF).astype(F32)
 
-    def await_windows(i):
+    def first_wave(i):
         for half in range(2):
             t_copy(i, half).wait_recv()
-
-    def first_wave(i):
-        pl.when(d == 1)(lambda: await_windows(i))
         (pr, pi), (tr, ti) = load(rolled, i), window(0, i)
         return rounded(
             right_left(pr * tr - pi * ti, pr * ti + pi * tr, tabs[2], tabs[3])
         )
 
     def far_field(i, wave):
-        pl.when(d == 0)(lambda: await_windows(i))
         (wr, wi), (tr, ti) = wave, window(1, i)
         fr, fi = right_left(wr * tr - wi * ti, wr * ti + wi * tr, tabs[0], tabs[1])
         used = jnp.where(jnp.full((1, WIN), own + i, jnp.int32) < counts[0], 1.0, 0.0)

time: 41.7 us -> 41.4 us (level)
  no operation moved by 1% of the time
where the time goes in v1:
time: 41.4 us; the launch traced here: 41.3 us
  Pallas kernels  40 us (97%)
  local copies, waits for them, and re-layouts  0.66 us (2%)
  between operations  0.66 us (2%)
    pallas_call x1, Pallas kernels, per_device(): pl.pallas_call(kernel, out_shape=pltpu.VMEM((2, 16, 1024), F32), in_specs...  40 us

profile of v1, /device:TPU:0, one launch (start us, length us, event | category | flops | bytes accessed | tf_op | source)
XLA Modules:
  0.0 41.3 jit_solution(17964585266822400558)
XLA Ops:
  0.7 40.0 %shard_map.64 = f32[2,16,1024]{2,1,0:T(8,128)S(1)} custom-call(s32[1]{0:T(128)S(6)} %copy.9.counts, s32[2,8]{1,0:T(2,128)} %bitcast.5, bf16[2,128,256]{2,1,0:T(8,128)(2,1)} %probe.1, f32[2,4,256,1024]{3,2,1,0:T(8,128)} %bitcast.4, f32[8,128,256]{2,1,0:T(8,128)} %measured.1, bf16[4,512,512]{2,1,0:T(8,128)(2,1)} %constant.2.clone.tabs_in), custom_call_target="tpu_custom_call" | custom-call | flops 4294967296 | bytes 12582912 | tf_op jit(solution)/shard_map/pallas_call | solution.py:387
  40.6 0.7 %copy.8 = f32[1,2,16,1024]{3,2,1,0:T(8,128)} copy(f32[1,2,16,1024]{3,2,1,0:T(8,128)S(1)} %bitcast.3) | data formatting | bytes 262144

commit v2 on v1

--- a/solution.py
+++ b/solution.py
@@ -15,7 +15,7 @@
 PLANE = 8
 CAP = 8
 CLS = 16
-ROUTE = ((2, 1), (2, 0), (0, 1), (1, 1), (3, 1), (1, 0), (3, 0), (0, 0))
+ROUTE = ((1, 0), (3, 0), (0, 1), (2, 0), (1, 1), (3, 1), (2, 1), (0, 0))
 MESH = pl.DeviceIdType.MESH
 BF = jnp.bfloat16
 F32 = jnp.float32
@@ -73,7 +73,7 @@
     counts, offs_in, probe, obj, measured, tabs_in, out,
     offs, other_offs, obj_v, tabs, t_all, t_send, probe_v, meas, rolled, amps, grad, pieces, places, acc, z_send, z_recv,
     load_sem, own_sem, probe_sem, meas_sem, t_sem, t_out_sem, out_sem, place_sem, place_out_sem,
-    piece_sem, piece_out_sem, z_sem, z_out_sem,
+    swap_sem, swap_out_sem, piece_sem, piece_out_sem, z_sem, z_out_sem,
 ):
     pos, d, c = lax.axis_index("pos"), lax.axis_index("depth"), lax.axis_index("det")
     z, q = pos // PLANE, pos % PLANE
@@ -99,10 +99,10 @@
     own_meas.start()
 
     barrier = pltpu.get_barrier_semaphore()
-    for k in range(1, 2 * CLS):
+    pl.semaphore_signal(barrier, inc=1, device_id=(pos, d, 1 - c), device_id_type=MESH)
+    for k in range(1, CLS):
         pl.semaphore_signal(
-            barrier, inc=1,
-            device_id=(z * PLANE + (q ^ (k // 4)), d ^ (k // 2 % 2), c ^ (k % 2)),
+            barrier, inc=1, device_id=(z * PLANE + (q ^ (k // 2)), d ^ (k % 2), c),
             device_id_type=MESH,
         )
     for k in range(1, BANDS):
@@ -118,7 +118,7 @@
             spread = jnp.where(slot_of == s, offs[axis, s], spread)
         places[q, axis] = spread
     acc[...] = jnp.zeros_like(acc)
-    pl.semaphore_wait(barrier, 2 * CLS - 1 + BANDS - 1)
+    pl.semaphore_wait(barrier, 1 + CLS - 1 + BANDS - 1)
 
     def place_copy(k):
         return pltpu.make_async_remote_copy(
@@ -224,32 +224,32 @@
         amps[i] = jnp.concatenate([meas[0, i], meas[1, i]], axis=0).T
     load_tabs.wait()
 
+    def swap(i, s):
+        part = grad.at[i, s, 1 - c, :, c]
+        return pltpu.make_async_remote_copy(
+            src_ref=part, dst_ref=part, send_sem=swap_out_sem.at[i, s], recv_sem=swap_sem.at[i, s],
+            device_id=(pos, d, 1 - c), device_id_type=MESH,
+        )
+
+    def piece_copy(i, s, yy, xx, out_sem):
+        return pltpu.make_async_remote_copy(
+            src_ref=grad.at[i, s, c, yy * 2 + xx // 2], dst_ref=pieces.at[i, q, d],
+            send_sem=out_sem, recv_sem=piece_sem.at[i, q],
+            device_id=(z * PLANE + yy * 2 + xx // 2, s, c), device_id_type=MESH,
+        )
+
     def send_pieces(i, s):
+        swap(i, s).wait_recv()
         odd = (s + d) % 2
-        for dy, far in ROUTE:
+        for dy, far in ROUTE[:-1]:
             yy = (y + dy * (1 + 2 * c)) % 4
             xx = (x + odd + 2 * ((far + c * odd) % 2)) % 4
-            for cc in range(2):
-                if (dy, far, cc) == (0, 0, 0):
-                    continue
-                core = c ^ cc
-                pltpu.make_async_remote_copy(
-                    src_ref=grad.at[i, s, (yy * 2 + xx // 2) * 2 + core],
-                    dst_ref=pieces.at[i, q, 2 * d + c],
-                    send_sem=piece_out_sem.at[i, s], recv_sem=piece_sem.at[i, q],
-                    device_id=(z * PLANE + yy * 2 + xx // 2, s, core), device_id_type=MESH,
-                ).start()
+            piece_copy(i, s, yy, xx, piece_out_sem.at[i, s]).start()
 
     def send_here(i):
-        xx = (x + 1 + 2 * c) % 4
-        pltpu.make_async_remote_copy(
-            src_ref=grad.at[i, 1 - d, (y * 2 + xx // 2) * 2 + c],
-            dst_ref=pieces.at[i, q, 2 * d + c],
-            send_sem=piece_out_sem.at[i, 0], recv_sem=piece_sem.at[i, q],
-            device_id=(z * PLANE + y * 2 + xx // 2, 1 - d, c), device_id_type=MESH,
-        ).start()
+        piece_copy(i, 1 - d, y, (x + 1 + 2 * c) % 4, piece_out_sem.at[i, 0]).start()
         pltpu.make_async_copy(
-            grad.at[i, d, cls], pieces.at[i, q, 2 * d + c], piece_sem.at[i, q]
+            grad.at[i, d, c, q], pieces.at[i, q, d], piece_sem.at[i, q]
         ).start()
 
     def load(ref, i):
@@ -278,8 +278,12 @@
 
     def put(i, s, wave, desc):
         (wr, wi), (dr, di) = wave, desc
-        grad[i, s, :, 0] = (wr * dr + wi * di).astype(BF).reshape(CLS, 16, WIN)
-        grad[i, s, :, 1] = (wr * di - wi * dr).astype(BF).reshape(CLS, 16, WIN)
+        re = (wr * dr + wi * di).astype(BF).reshape(PLANE, 2, 16, WIN)
+        im = (wr * di - wi * dr).astype(BF).reshape(PLANE, 2, 16, WIN)
+        for core in range(2):
+            grad[i, s, core, :, c, 0] = re[:, core]
+            grad[i, s, core, :, c, 1] = im[:, core]
+        swap(i, s).start()
 
     def first_descent(i, desc):
         (dr, di), (tr, ti) = desc, window(1, i)
@@ -290,16 +294,15 @@
     wave_a = first_wave(0)
     desc_a = descent(far_field(0, wave_a))
     put(0, 1, wave_a, desc_a)
+    put(0, 0, load(rolled, 0), first_descent(0, desc_a))
     send_pieces(0, 1)
     wave_b = first_wave(1)
-    desc_a = first_descent(0, desc_a)
-    put(0, 0, load(rolled, 0), desc_a)
     send_pieces(0, 0)
     send_here(0)
     desc_b = descent(far_field(1, wave_b))
     put(1, 1, wave_b, desc_b)
+    put(1, 0, load(rolled, 1), first_descent(1, desc_b))
     send_pieces(1, 1)
-    put(1, 0, load(rolled, 1), first_descent(1, desc_b))
     send_pieces(1, 0)
     send_here(1)
 
@@ -320,7 +323,7 @@
         band = [wide(r0, k) + jnp.where(row16 < wide(rm, k), 1, 0) for k in range(4)]
         block = [wide(c0, k) + jnp.where(col8 < wide(cm, k), 1, 0) for k in range(4)]
         for p in range(2):
-            piece = [pieces[i, g, k, p].astype(F32).reshape(2, 8, WIN) for k in range(4)]
+            piece = [pieces[i, g, k // 2, k % 2, p].astype(F32).reshape(2, 8, WIN) for k in range(4)]
             for zb in range(BANDS):
                 part = [jnp.where(b == zb, x, 0.0) for b, x in zip(band, piece)]
                 for cb in range(BANDS):
@@ -373,8 +376,9 @@
     for k in range(1, PLANE):
         place_copy(k).wait_send()
     for i in range(2):
-        for s, count in ((0, CLS), (1, CLS - 1)):
-            sent = grad.at[i, s, pl.ds(0, count)]
+        for s, count in ((0, PLANE), (1, PLANE - 1)):
+            swap(i, s).wait_send()
+            sent = grad.at[i, s, 0, pl.ds(0, count)]
             pltpu.make_async_copy(sent, sent, piece_out_sem.at[i, s]).wait()
 
 
@@ -400,8 +404,8 @@
             pltpu.VMEM((2, 2, WIN // 2, WIN), F32),
             pltpu.VMEM((2, 2, WIN, WIN), BF),
             pltpu.VMEM((2, WIN, WIN), F32),
-            pltpu.VMEM((2, 2, CLS, 2, 16, WIN), BF),
-            pltpu.VMEM((2, PLANE, CAP // 2, 2, 16, WIN), BF),
+            pltpu.VMEM((2, 2, 2, PLANE, 2, 2, 16, WIN), BF),
+            pltpu.VMEM((2, PLANE, 2, 2, 2, 16, WIN), BF),
             pltpu.VMEM((PLANE, 2, CAP, 128), jnp.int32),
             pltpu.VMEM((BANDS, 2, 2, 8, 1024), F32),
             pltpu.VMEM((BANDS, 2, 16, 1024), BF),
@@ -415,6 +419,8 @@
             dma((2,)),
             dma((PLANE,)),
             dma((PLANE,)),
+            dma((2, 2)),
+            dma((2, 2)),
             dma((2, PLANE)),
             dma((2, 2)),
             dma((BANDS,)),

time: 41.4 us -> 43.4 us (1.048)
  Pallas kernels: 40 us -> 42 us
    pallas_call x1, Pallas kernels: 40 us -> 42 us  [per_device(): pl.pallas_call(kernel, out_shape=pltpu.VMEM((2, 16, 1024), F32), in_specs...]
where the time goes in v2:
time: 43.4 us; the launch traced here: 43.3 us
  Pallas kernels  42 us (97%)
  local copies, waits for them, and re-layouts  0.66 us (2%)
  between operations  0.66 us (2%)
    pallas_call x1, Pallas kernels, per_device(): pl.pallas_call(kernel, out_shape=pltpu.VMEM((2, 16, 1024), F32), in_specs...  42 us

profile of v2, /device:TPU:0, one launch (start us, length us, event | category | flops | bytes accessed | tf_op | source)
XLA Modules:
  0.0 43.3 jit_solution(10961723783838470291)
XLA Ops:
  0.7 42.0 %shard_map.64 = f32[2,16,1024]{2,1,0:T(8,128)S(1)} custom-call(s32[1]{0:T(128)S(6)} %copy.9.counts, s32[2,8]{1,0:T(2,128)} %bitcast.5, bf16[2,128,256]{2,1,0:T(8,128)(2,1)} %probe.1, f32[2,4,256,1024]{3,2,1,0:T(8,128)} %bitcast.4, f32[8,128,256]{2,1,0:T(8,128)} %measured.1, bf16[4,512,512]{2,1,0:T(8,128)(2,1)} %constant.2.clone.tabs_in), custom_call_target="tpu_custom_call" | custom-call | flops 4294967296 | bytes 12582912 | tf_op jit(solution)/shard_map/pallas_call | solution.py:391
  42.7 0.7 %copy.8 = f32[1,2,16,1024]{3,2,1,0:T(8,128)} copy(f32[1,2,16,1024]{3,2,1,0:T(8,128)S(1)} %bitcast.3) | data formatting | bytes 262144

commit v3 on v1

--- a/solution.py
+++ b/solution.py
@@ -15,7 +15,7 @@
 PLANE = 8
 CAP = 8
 CLS = 16
-ROUTE = ((2, 1), (2, 0), (0, 1), (1, 1), (3, 1), (1, 0), (3, 0), (0, 0))
+ROUTE = ((1, 0), (3, 0), (0, 1), (2, 0), (1, 1), (3, 1), (2, 1), (0, 0))
 MESH = pl.DeviceIdType.MESH
 BF = jnp.bfloat16
 F32 = jnp.float32
@@ -91,24 +91,24 @@
         column = obj.at[:, :, :, pl.ds(cb * WIN, WIN)]
         load_obj.append(pltpu.make_async_copy(column, obj_v.at[cb], load_sem.at[cb]))
         load_obj[-1].start()
+    barrier = pltpu.get_barrier_semaphore()
+    for k in range(1, 2 * CLS):
+        pl.semaphore_signal(
+            barrier, inc=1,
+            device_id=(z * PLANE + (q ^ (k // 4)), d ^ (k // 2 % 2), c ^ (k % 2)),
+            device_id_type=MESH,
+        )
+    for k in range(1, BANDS):
+        pl.semaphore_signal(
+            barrier, inc=1, device_id=((z + k) % BANDS * PLANE + q, d, c), device_id_type=MESH
+        )
+
     load_tabs = pltpu.make_async_copy(tabs_in, tabs, load_sem.at[BANDS])
     load_tabs.start()
     own_probe = pltpu.make_async_copy(probe, probe_v.at[c], own_sem.at[0])
     own_probe.start()
     own_meas = pltpu.make_async_copy(measured.at[pl.ds(own, 2)], meas.at[c], own_sem.at[1])
     own_meas.start()
-
-    barrier = pltpu.get_barrier_semaphore()
-    for k in range(1, 2 * CLS):
-        pl.semaphore_signal(
-            barrier, inc=1,
-            device_id=(z * PLANE + (q ^ (k // 4)), d ^ (k // 2 % 2), c ^ (k % 2)),
-            device_id_type=MESH,
-        )
-    for k in range(1, BANDS):
-        pl.semaphore_signal(
-            barrier, inc=1, device_id=((z + k) % BANDS * PLANE + q, d, c), device_id_type=MESH
-        )
 
     own_offs.wait()
     slot_of = iota((CAP, 128), 0)
@@ -130,7 +130,11 @@
     def places_of(g):
         return pltpu.make_async_copy(places.at[g], places.at[g], place_sem.at[g])
 
-    place_copy(1).start()
+    offs_copy = pltpu.make_async_remote_copy(
+        src_ref=offs, dst_ref=other_offs, send_sem=place_out_sem.at[0], recv_sem=own_sem.at[2],
+        device_id=(other, d, c), device_id_type=MESH,
+    )
+    offs_copy.start()
 
     probe_copy = pltpu.make_async_remote_copy(
         src_ref=probe, dst_ref=probe_v.at[c], send_sem=out_sem.at[0], recv_sem=probe_sem,
@@ -172,22 +176,24 @@
             device_id=(there, 1 - d, c), device_id_type=MESH,
         )
 
-    places_of(q ^ 1).wait()
-    fetch = pltpu.make_async_copy(places.at[q ^ 1], other_offs, own_sem.at[2])
-    fetch.start()
-    fetch.wait()
-
-    def send_half(n, carry):
-        i, half = n // 2, (n + c) % 2
-        r = jnp.where(half == 1, other_offs[0, across + i, 0], offs[0, across + i])
-        col = jnp.where(half == 1, other_offs[1, across + i, 0], offs[1, across + i])
+    def send_near(i):
         for plane in range(2):
-            t_send[i, half, plane] = cut(r, col, half, plane)
-        t_copy(i, half).start()
-        return carry
-
-    lax.fori_loop(0, 4, send_half, 0)
-    for k in range(2, PLANE):
+            t_send[i, 0, plane] = cut(offs[0, across + i], offs[1, across + i], 0, plane)
+        t_copy(i, 0).start()
+
+    def send_far(i):
+        for plane in range(2):
+            t_send[i, 1, plane] = cut(
+                other_offs[0, across + i], other_offs[1, across + i], 1, plane
+            )
+        t_copy(i, 1).start()
+
+    send_near(0)
+    offs_copy.wait_recv()
+    send_far(0)
+    send_near(1)
+    send_far(1)
+    for k in range(1, PLANE):
         place_copy(k).start()
 
     def cut_own(i, carry):
@@ -332,7 +338,7 @@
     def add_first(k, carry):
         g = q ^ k ^ (k // 4 * 2)
 
-        @pl.when(k > 1)
+        @pl.when(k > 0)
         def _():
             places_of(g).wait()
 
@@ -365,6 +371,7 @@
 
     for k in range(1, BANDS):
         z_copy(k).wait_send()
+    offs_copy.wait_send()
     probe_copy.wait_send()
     meas_copy.wait_send()
     for i in range(2):
@@ -391,7 +398,7 @@
         out_specs=pl.BlockSpec(memory_space=pltpu.VMEM),
         scratch_shapes=[
             pltpu.SMEM((2, CAP), jnp.int32),
-            pltpu.SMEM((2, CAP, 128), jnp.int32),
+            pltpu.SMEM((2, CAP), jnp.int32),
             pltpu.VMEM((BANDS, 2, BANDS, WIN, WIN), F32),
             pltpu.VMEM((4, 2 * WIN, 2 * WIN), BF),
             pltpu.VMEM((2, 2, 2, 2, HALF, WIN), BF),

time: 41.4 us -> 39.9 us (0.964)
  Pallas kernels: 40 us -> 38.5 us
    pallas_call x1, Pallas kernels: 40 us -> 38.5 us  [per_device(): pl.pallas_call(kernel, out_shape=pltpu.VMEM((2, 16, 1024), F32), in_specs...]
where the time goes in v3:
time: 39.9 us; the launch traced here: 39.8 us
  Pallas kernels  38.5 us (96%)
  local copies, waits for them, and re-layouts  0.66 us (2%)
  between operations  0.66 us (2%)
    pallas_call x1, Pallas kernels, per_device(): pl.pallas_call(kernel, out_shape=pltpu.VMEM((2, 16, 1024), F32), in_specs...  38.5 us

profile of v3, /device:TPU:0, one launch (start us, length us, event | category | flops | bytes accessed | tf_op | source)
XLA Modules:
  0.0 39.8 jit_solution(1120168077511052130)
XLA Ops:
  0.7 38.5 %shard_map.64 = f32[2,16,1024]{2,1,0:T(8,128)S(1)} custom-call(s32[1]{0:T(128)S(6)} %copy.9.counts, s32[2,8]{1,0:T(2,128)} %bitcast.5, bf16[2,128,256]{2,1,0:T(8,128)(2,1)} %probe.1, f32[2,4,256,1024]{3,2,1,0:T(8,128)} %bitcast.4, f32[8,128,256]{2,1,0:T(8,128)} %measured.1, bf16[4,512,512]{2,1,0:T(8,128)(2,1)} %constant.2.clone.tabs_in), custom_call_target="tpu_custom_call" | custom-call | flops 4294967296 | bytes 12582912 | tf_op jit(solution)/shard_map/pallas_call | solution.py:394
  39.1 0.7 %copy.8 = f32[1,2,16,1024]{3,2,1,0:T(8,128)} copy(f32[1,2,16,1024]{3,2,1,0:T(8,128)S(1)} %bitcast.3) | data formatting | bytes 262144

commit v4 on v3

--- a/solution.py
+++ b/solution.py
@@ -11,6 +11,8 @@
 PROP_DIV = 2
 WIN = 256
 HALF = WIN // 2
+NEAR = 160
+PARTS = ((0, NEAR), (NEAR, WIN - NEAR))
 BANDS = 4
 PLANE = 8
 CAP = 8
@@ -152,75 +154,50 @@
 
     row_of, col_of = iota((WIN, WIN), 0), iota((WIN, WIN), 1)
 
-    half_row = iota((HALF, WIN), 0)
-    half_col = iota((HALF, WIN), 1)
-
-    def cut(r, col, half, plane):
-        rows = pl.ds(half * HALF, HALF)
+    def cut(r, col, plane, first, count):
+        rows = pl.ds(first, count)
         band = jnp.minimum(r >> 8, BANDS - 2)
         block = jnp.minimum(col >> 8, BANDS - 2)
-        late = half_col >= col - block * WIN
+        late = iota((count, WIN), 1) >= col - block * WIN
         top = jnp.where(
             late, obj_v[block, plane, band, rows], obj_v[block + 1, plane, band, rows]
         )
         low = jnp.where(
             late, obj_v[block, plane, band + 1, rows], obj_v[block + 1, plane, band + 1, rows]
         )
-        return jnp.where(half_row >= r - band * WIN - half * HALF, top, low).astype(BF)
-
-    def t_copy(i, half):
-        there = pos + half * (other - pos)
+        return jnp.where(iota((count, WIN), 0) >= r - band * WIN - first, top, low).astype(BF)
+
+    def t_copy(i, part):
+        rows = pl.ds(*PARTS[part])
         return pltpu.make_async_remote_copy(
-            src_ref=t_send.at[i, half], dst_ref=t_all.at[d, i, half],
-            send_sem=t_out_sem.at[i, half], recv_sem=t_sem.at[i, half],
-            device_id=(there, 1 - d, c), device_id_type=MESH,
-        )
-
-    def send_near(i):
+            src_ref=t_send.at[i, :, rows], dst_ref=t_all.at[d, i, :, rows],
+            send_sem=t_out_sem.at[i, part], recv_sem=t_sem.at[i, part],
+            device_id=(other if part else pos, 1 - d, c), device_id_type=MESH,
+        )
+
+    def send_part(i, part):
+        places_in = other_offs if part else offs
         for plane in range(2):
-            t_send[i, 0, plane] = cut(offs[0, across + i], offs[1, across + i], 0, plane)
-        t_copy(i, 0).start()
-
-    def send_far(i):
+            t_send[i, plane, pl.ds(*PARTS[part])] = cut(
+                places_in[0, across + i], places_in[1, across + i], plane, *PARTS[part]
+            )
+        t_copy(i, part).start()
+
+    send_part(0, 0)
+    offs_copy.wait_recv()
+    send_part(0, 1)
+    send_part(1, 0)
+    send_part(1, 1)
+
+    def window(s, i):
+        return [t_all[s, i, p].astype(F32) for p in range(2)]
+
+    def prepare(i):
         for plane in range(2):
-            t_send[i, 1, plane] = cut(
-                other_offs[0, across + i], other_offs[1, across + i], 1, plane
-            )
-        t_copy(i, 1).start()
-
-    send_near(0)
-    offs_copy.wait_recv()
-    send_far(0)
-    send_near(1)
-    send_far(1)
-    for k in range(1, PLANE):
-        place_copy(k).start()
-
-    def cut_own(i, carry):
-        for half in range(2):
-            for plane in range(2):
-                t_all[d, i, half, plane] = cut(
-                    offs[0, own + i], offs[1, own + i], half, plane
-                )
-        return carry
-
-    lax.fori_loop(0, 2, cut_own, 0)
-
-    def window(s, i):
-        return [
-            jnp.concatenate([t_all[s, i, 0, p], t_all[s, i, 1, p]], axis=0).astype(F32)
-            for p in range(2)
-        ]
-
-    own_probe.wait()
-    own_meas.wait()
-    probe_copy.wait_recv()
-    meas_copy.wait_recv()
-
-    flat = jnp.concatenate(
-        [jnp.concatenate([probe_v[0, p], probe_v[1, p]], axis=0) for p in range(2)], axis=1
-    )
-    for i in range(2):
+            t_all[d, i, plane] = cut(offs[0, own + i], offs[1, own + i], plane, 0, WIN)
+        flat = jnp.concatenate(
+            [jnp.concatenate([probe_v[0, p], probe_v[1, p]], axis=0) for p in range(2)], axis=1
+        )
         r, col = offs[0, own + i], offs[1, own + i]
         down = jnp.where(col_of == ((row_of - r) & (WIN - 1)), 1.0, 0.0).astype(BF)
         over = jnp.where(row_of == ((col_of - col) & (WIN - 1)), 1.0, 0.0).astype(BF)
@@ -228,6 +205,12 @@
         moved = dot(jnp.concatenate([moved[:, :WIN], moved[:, WIN:]], axis=0), over)
         rolled[i, 0], rolled[i, 1] = moved[:WIN].astype(BF), moved[WIN:].astype(BF)
         amps[i] = jnp.concatenate([meas[0, i], meas[1, i]], axis=0).T
+
+    own_probe.wait()
+    own_meas.wait()
+    probe_copy.wait_recv()
+    meas_copy.wait_recv()
+    prepare(0)
     load_tabs.wait()
 
     def send_pieces(i, s):
@@ -297,6 +280,9 @@
     desc_a = descent(far_field(0, wave_a))
     put(0, 1, wave_a, desc_a)
     send_pieces(0, 1)
+    for k in range(1, PLANE):
+        place_copy(k).start()
+    prepare(1)
     wave_b = first_wave(1)
     desc_a = first_descent(0, desc_a)
     put(0, 0, load(rolled, 0), desc_a)
@@ -401,8 +387,8 @@
             pltpu.SMEM((2, CAP), jnp.int32),
             pltpu.VMEM((BANDS, 2, BANDS, WIN, WIN), F32),
             pltpu.VMEM((4, 2 * WIN, 2 * WIN), BF),
-            pltpu.VMEM((2, 2, 2, 2, HALF, WIN), BF),
-            pltpu.VMEM((2, 2, 2, HALF, WIN), BF),
+            pltpu.VMEM((2, 2, 2, WIN, WIN), BF),
+            pltpu.VMEM((2, 2, WIN, WIN), BF),
             pltpu.VMEM((2, 2, WIN // 2, WIN), BF),
             pltpu.VMEM((2, 2, WIN // 2, WIN), F32),
             pltpu.VMEM((2, 2, WIN, WIN), BF),

time: 39.9 us -> 40.1 us (level)
  no operation moved by 1% of the time
where the time goes in v4:
time: 40.1 us; the launch traced here: 40 us
  Pallas kernels  38.7 us (97%)
  local copies, waits for them, and re-layouts  0.66 us (2%)
  between operations  0.66 us (2%)
    pallas_call x1, Pallas kernels, per_device(): pl.pallas_call(kernel, out_shape=pltpu.VMEM((2, 16, 1024), F32), in_specs...  38.7 us

profile of v4, /device:TPU:0, one launch (start us, length us, event | category | flops | bytes accessed | tf_op | source)
XLA Modules:
  0.0 40.0 jit_solution(15273769472649416848)
XLA Ops:
  0.7 38.7 %shard_map.64 = f32[2,16,1024]{2,1,0:T(8,128)S(1)} custom-call(s32[1]{0:T(128)S(6)} %copy.9.counts, s32[2,8]{1,0:T(2,128)} %bitcast.5, bf16[2,128,256]{2,1,0:T(8,128)(2,1)} %probe.1, f32[2,4,256,1024]{3,2,1,0:T(8,128)} %bitcast.4, f32[8,128,256]{2,1,0:T(8,128)} %measured.1, bf16[4,512,512]{2,1,0:T(8,128)(2,1)} %constant.2.clone.tabs_in), custom_call_target="tpu_custom_call" | custom-call | flops 4294967296 | bytes 12582912 | tf_op jit(solution)/shard_map/pallas_call | solution.py:380
  39.3 0.7 %copy.8 = f32[1,2,16,1024]{3,2,1,0:T(8,128)} copy(f32[1,2,16,1024]{3,2,1,0:T(8,128)S(1)} %bitcast.3) | data formatting | bytes 262144

commit v5 on v4

--- a/solution.py
+++ b/solution.py
@@ -211,6 +211,9 @@
     probe_copy.wait_recv()
     meas_copy.wait_recv()
     prepare(0)
+    prepare(1)
+    for k in range(1, PLANE):
+        place_copy(k).start()
     load_tabs.wait()
 
     def send_pieces(i, s):
@@ -280,9 +283,6 @@
     desc_a = descent(far_field(0, wave_a))
     put(0, 1, wave_a, desc_a)
     send_pieces(0, 1)
-    for k in range(1, PLANE):
-        place_copy(k).start()
-    prepare(1)
     wave_b = first_wave(1)
     desc_a = first_descent(0, desc_a)
     put(0, 0, load(rolled, 0), desc_a)
@@ -290,10 +290,10 @@
     send_here(0)
     desc_b = descent(far_field(1, wave_b))
     put(1, 1, wave_b, desc_b)
-    send_pieces(1, 1)
     put(1, 0, load(rolled, 1), first_descent(1, desc_b))
     send_pieces(1, 0)
     send_here(1)
+    send_pieces(1, 1)
 
     row16 = iota((2, 8, WIN), 0) * 8 + iota((2, 8, WIN), 1) + cls * 16
     col8 = iota((8, WIN), 1)

time: 40.1 us -> 40.2 us (level); the launches traced: 40 us -> 39.7 us
  no operation moved by 1% of the time
where the time goes in v5:
time: 40.2 us; the launch traced here: 39.7 us
  Pallas kernels  38.3 us (95%)
  local copies, waits for them, and re-layouts  0.66 us (2%)
  between operations  0.66 us (2%)
    pallas_call x1, Pallas kernels, per_device(): pl.pallas_call(kernel, out_shape=pltpu.VMEM((2, 16, 1024), F32), in_specs...  38.3 us

profile of v5, /device:TPU:0, one launch (start us, length us, event | category | flops | bytes accessed | tf_op | source)
XLA Modules:
  0.0 39.7 jit_solution(9106483966666680123)
XLA Ops:
  0.7 38.3 %shard_map.64 = f32[2,16,1024]{2,1,0:T(8,128)S(1)} custom-call(s32[1]{0:T(128)S(6)} %copy.9.counts, s32[2,8]{1,0:T(2,128)} %bitcast.5, bf16[2,128,256]{2,1,0:T(8,128)(2,1)} %probe.1, f32[2,4,256,1024]{3,2,1,0:T(8,128)} %bitcast.4, f32[8,128,256]{2,1,0:T(8,128)} %measured.1, bf16[4,512,512]{2,1,0:T(8,128)(2,1)} %constant.2.clone.tabs_in), custom_call_target="tpu_custom_call" | custom-call | flops 4294967296 | bytes 12582912 | tf_op jit(solution)/shard_map/pallas_call | solution.py:380
  39.0 0.7 %copy.8 = f32[1,2,16,1024]{3,2,1,0:T(8,128)} copy(f32[1,2,16,1024]{3,2,1,0:T(8,128)S(1)} %bitcast.3) | data formatting | bytes 262144

commit v6 on v3

--- a/solution.py
+++ b/solution.py
@@ -78,6 +78,7 @@
     pos, d, c = lax.axis_index("pos"), lax.axis_index("depth"), lax.axis_index("det")
     z, q = pos // PLANE, pos % PLANE
     y, x = q // 2, q % 2 * 2 + d
+    first_of_plane = z * PLANE
     cls = q * 2 + c
     other = z * PLANE + (q ^ 1)
     own = 2 * (2 * d + c)
@@ -231,19 +232,21 @@
     load_tabs.wait()
 
     def send_pieces(i, s):
-        odd = (s + d) % 2
+        odd = d ^ s
+        flip = c & odd
         for dy, far in ROUTE:
-            yy = (y + dy * (1 + 2 * c)) % 4
-            xx = (x + odd + 2 * ((far + c * odd) % 2)) % 4
+            yy = (y + (dy if dy % 2 == 0 else dy + 2 * c)) & 3
+            xh = ((x + odd + 2 * (far ^ flip)) & 3) >> 1
+            group = yy * 2 + xh
             for cc in range(2):
                 if (dy, far, cc) == (0, 0, 0):
                     continue
                 core = c ^ cc
                 pltpu.make_async_remote_copy(
-                    src_ref=grad.at[i, s, (yy * 2 + xx // 2) * 2 + core],
+                    src_ref=grad.at[i, s, group * 2 + core],
                     dst_ref=pieces.at[i, q, 2 * d + c],
                     send_sem=piece_out_sem.at[i, s], recv_sem=piece_sem.at[i, q],
-                    device_id=(z * PLANE + yy * 2 + xx // 2, s, core), device_id_type=MESH,
+                    device_id=(first_of_plane + group, s, core), device_id_type=MESH,
                 ).start()
 
     def send_here(i):
@@ -361,10 +364,10 @@
             recv_sem=z_sem.at[k], device_id=(there * PLANE + q, d, c), device_id_type=MESH,
         )
 
-    for k in (1 + 2 * c, 3 - 2 * c, 2):
+    for k in (1 + c, 2 - c, 3):
         z_copy(k).start()
     total = acc[z].reshape(2, 16, 1024)
-    for k in (1, 3, 2):
+    for k in (3, 2, 1):
         z_copy(k).wait_recv()
         total += z_recv[k].astype(F32)
     out[...] = total

time: 39.9 us -> 39.7 us (level)
  no operation moved by 1% of the time
where the time goes in v6:
time: 39.7 us; the launch traced here: 39.6 us
  Pallas kernels  38.3 us (96%)
  local copies, waits for them, and re-layouts  0.66 us (2%)
  between operations  0.66 us (2%)
    pallas_call x1, Pallas kernels, per_device(): pl.pallas_call(kernel, out_shape=pltpu.VMEM((2, 16, 1024), F32), in_specs...  38.3 us

profile of v6, /device:TPU:0, one launch (start us, length us, event | category | flops | bytes accessed | tf_op | source)
XLA Modules:
  0.0 39.6 jit_solution(17942759930346068373)
XLA Ops:
  0.7 38.3 %shard_map.64 = f32[2,16,1024]{2,1,0:T(8,128)S(1)} custom-call(s32[1]{0:T(128)S(6)} %copy.9.counts, s32[2,8]{1,0:T(2,128)} %bitcast.5, bf16[2,128,256]{2,1,0:T(8,128)(2,1)} %probe.1, f32[2,4,256,1024]{3,2,1,0:T(8,128)} %bitcast.4, f32[8,128,256]{2,1,0:T(8,128)} %measured.1, bf16[4,512,512]{2,1,0:T(8,128)(2,1)} %constant.2.clone.tabs_in), custom_call_target="tpu_custom_call" | custom-call | flops 4294967296 | bytes 12582912 | tf_op jit(solution)/shard_map/pallas_call | solution.py:397
  38.9 0.7 %copy.8 = f32[1,2,16,1024]{3,2,1,0:T(8,128)} copy(f32[1,2,16,1024]{3,2,1,0:T(8,128)S(1)} %bitcast.3) | data formatting | bytes 262144

commit v7 on v5

--- a/solution.py
+++ b/solution.py
@@ -80,6 +80,7 @@
     pos, d, c = lax.axis_index("pos"), lax.axis_index("depth"), lax.axis_index("det")
     z, q = pos // PLANE, pos % PLANE
     y, x = q // 2, q % 2 * 2 + d
+    first_of_plane = z * PLANE
     cls = q * 2 + c
     other = z * PLANE + (q ^ 1)
     own = 2 * (2 * d + c)
@@ -211,25 +212,26 @@
     probe_copy.wait_recv()
     meas_copy.wait_recv()
     prepare(0)
-    prepare(1)
     for k in range(1, PLANE):
         place_copy(k).start()
     load_tabs.wait()
 
     def send_pieces(i, s):
-        odd = (s + d) % 2
+        odd = d ^ s
+        flip = c & odd
         for dy, far in ROUTE:
-            yy = (y + dy * (1 + 2 * c)) % 4
-            xx = (x + odd + 2 * ((far + c * odd) % 2)) % 4
+            yy = (y + (dy if dy % 2 == 0 else dy + 2 * c)) & 3
+            xh = ((x + odd + 2 * (far ^ flip)) & 3) >> 1
+            group = yy * 2 + xh
             for cc in range(2):
                 if (dy, far, cc) == (0, 0, 0):
                     continue
                 core = c ^ cc
                 pltpu.make_async_remote_copy(
-                    src_ref=grad.at[i, s, (yy * 2 + xx // 2) * 2 + core],
+                    src_ref=grad.at[i, s, group * 2 + core],
                     dst_ref=pieces.at[i, q, 2 * d + c],
                     send_sem=piece_out_sem.at[i, s], recv_sem=piece_sem.at[i, q],
-                    device_id=(z * PLANE + yy * 2 + xx // 2, s, core), device_id_type=MESH,
+                    device_id=(first_of_plane + group, s, core), device_id_type=MESH,
                 ).start()
 
     def send_here(i):
@@ -280,6 +282,7 @@
         )
 
     wave_a = first_wave(0)
+    prepare(1)
     desc_a = descent(far_field(0, wave_a))
     put(0, 1, wave_a, desc_a)
     send_pieces(0, 1)
@@ -290,10 +293,10 @@
     send_here(0)
     desc_b = descent(far_field(1, wave_b))
     put(1, 1, wave_b, desc_b)
+    send_pieces(1, 1)
     put(1, 0, load(rolled, 1), first_descent(1, desc_b))
     send_pieces(1, 0)
     send_here(1)
-    send_pieces(1, 1)
 
     row16 = iota((2, 8, WIN), 0) * 8 + iota((2, 8, WIN), 1) + cls * 16
     col8 = iota((8, WIN), 1)
@@ -347,10 +350,10 @@
             recv_sem=z_sem.at[k], device_id=(there * PLANE + q, d, c), device_id_type=MESH,
         )
 
-    for k in (1 + 2 * c, 3 - 2 * c, 2):
+    for k in (1 + c, 2 - c, 3):
         z_copy(k).start()
     total = acc[z].reshape(2, 16, 1024)
-    for k in (1, 3, 2):
+    for k in (3, 2, 1):
         z_copy(k).wait_recv()
         total += z_recv[k].astype(F32)
     out[...] = total

time: 40.2 us -> 39.7 us (0.988)
  no operation moved by 1% of the time
where the time goes in v7:
time: 39.7 us; the launch traced here: 39.3 us
  Pallas kernels  38 us (96%)
  local copies, waits for them, and re-layouts  0.66 us (2%)
  between operations  0.66 us (2%)
    pallas_call x1, Pallas kernels, per_device(): pl.pallas_call(kernel, out_shape=pltpu.VMEM((2, 16, 1024), F32), in_specs...  38 us

profile of v7, /device:TPU:0, one launch (start us, length us, event | category | flops | bytes accessed | tf_op | source)
XLA Modules:
  0.0 39.3 jit_solution(15933002928662777391)
XLA Ops:
  0.7 38.0 %shard_map.64 = f32[2,16,1024]{2,1,0:T(8,128)S(1)} custom-call(s32[1]{0:T(128)S(6)} %copy.9.counts, s32[2,8]{1,0:T(2,128)} %bitcast.5, bf16[2,128,256]{2,1,0:T(8,128)(2,1)} %probe.1, f32[2,4,256,1024]{3,2,1,0:T(8,128)} %bitcast.4, f32[8,128,256]{2,1,0:T(8,128)} %measured.1, bf16[4,512,512]{2,1,0:T(8,128)(2,1)} %constant.2.clone.tabs_in), custom_call_target="tpu_custom_call" | custom-call | flops 4294967296 | bytes 12582912 | tf_op jit(solution)/shard_map/pallas_call | solution.py:383
  38.7 0.7 %copy.8 = f32[1,2,16,1024]{3,2,1,0:T(8,128)} copy(f32[1,2,16,1024]{3,2,1,0:T(8,128)S(1)} %bitcast.3) | data formatting | bytes 262144

commit v8 on v7

--- a/solution.py
+++ b/solution.py
@@ -293,10 +293,10 @@
     send_here(0)
     desc_b = descent(far_field(1, wave_b))
     put(1, 1, wave_b, desc_b)
-    send_pieces(1, 1)
     put(1, 0, load(rolled, 1), first_descent(1, desc_b))
     send_pieces(1, 0)
     send_here(1)
+    send_pieces(1, 1)
 
     row16 = iota((2, 8, WIN), 0) * 8 + iota((2, 8, WIN), 1) + cls * 16
     col8 = iota((8, WIN), 1)

time: 39.7 us -> 39.8 us (level)
  no operation moved by 1% of the time
where the time goes in v8:
time: 39.8 us; the launch traced here: 39.4 us
  Pallas kernels  38.1 us (96%)
  local copies, waits for them, and re-layouts  0.66 us (2%)
  between operations  0.66 us (2%)
    pallas_call x1, Pallas kernels, per_device(): pl.pallas_call(kernel, out_shape=pltpu.VMEM((2, 16, 1024), F32), in_specs...  38.1 us

profile of v8, /device:TPU:0, one launch (start us, length us, event | category | flops | bytes accessed | tf_op | source)
XLA Modules:
  0.0 39.4 jit_solution(12282934133041211186)
XLA Ops:
  0.7 38.1 %shard_map.64 = f32[2,16,1024]{2,1,0:T(8,128)S(1)} custom-call(s32[1]{0:T(128)S(6)} %copy.9.counts, s32[2,8]{1,0:T(2,128)} %bitcast.5, bf16[2,128,256]{2,1,0:T(8,128)(2,1)} %probe.1, f32[2,4,256,1024]{3,2,1,0:T(8,128)} %bitcast.4, f32[8,128,256]{2,1,0:T(8,128)} %measured.1, bf16[4,512,512]{2,1,0:T(8,128)(2,1)} %constant.2.clone.tabs_in), custom_call_target="tpu_custom_call" | custom-call | flops 4294967296 | bytes 12582912 | tf_op jit(solution)/shard_map/pallas_call | solution.py:383
  38.8 0.7 %copy.8 = f32[1,2,16,1024]{3,2,1,0:T(8,128)} copy(f32[1,2,16,1024]{3,2,1,0:T(8,128)S(1)} %bitcast.3) | data formatting | bytes 262144

commit v9 on v7

--- a/solution.py
+++ b/solution.py
@@ -87,6 +87,18 @@
     across = 2 * (2 * (1 - d) + c)
     beside_slot = 2 * (2 * d + 1 - c)
 
+    barrier = pltpu.get_barrier_semaphore()
+    for k in range(1, 2 * CLS):
+        pl.semaphore_signal(
+            barrier, inc=1,
+            device_id=(z * PLANE + (q ^ (k // 4)), d ^ (k // 2 % 2), c ^ (k % 2)),
+            device_id_type=MESH,
+        )
+    for k in range(1, BANDS):
+        pl.semaphore_signal(
+            barrier, inc=1, device_id=((z + k) % BANDS * PLANE + q, d, c), device_id_type=MESH
+        )
+
     own_offs = pltpu.make_async_copy(offs_in, offs, own_sem.at[3])
     own_offs.start()
     load_obj = []
@@ -94,18 +106,6 @@
         column = obj.at[:, :, :, pl.ds(cb * WIN, WIN)]
         load_obj.append(pltpu.make_async_copy(column, obj_v.at[cb], load_sem.at[cb]))
         load_obj[-1].start()
-    barrier = pltpu.get_barrier_semaphore()
-    for k in range(1, 2 * CLS):
-        pl.semaphore_signal(
-            barrier, inc=1,
-            device_id=(z * PLANE + (q ^ (k // 4)), d ^ (k // 2 % 2), c ^ (k % 2)),
-            device_id_type=MESH,
-        )
-    for k in range(1, BANDS):
-        pl.semaphore_signal(
-            barrier, inc=1, device_id=((z + k) % BANDS * PLANE + q, d, c), device_id_type=MESH
-        )
-
     load_tabs = pltpu.make_async_copy(tabs_in, tabs, load_sem.at[BANDS])
     load_tabs.start()
     own_probe = pltpu.make_async_copy(probe, probe_v.at[c], own_sem.at[0])
@@ -341,8 +341,6 @@
     lax.fori_loop(0, PLANE, add_first, 0)
     lax.fori_loop(0, PLANE, add_second, 0)
 
-    z_send[...] = acc[...].reshape(BANDS, 2, 16, 1024).astype(BF)
-
     def z_copy(k):
         there = (z + k) % BANDS
         return pltpu.make_async_remote_copy(
@@ -351,6 +349,7 @@
         )
 
     for k in (1 + c, 2 - c, 3):
+        z_send[(z + k) % BANDS] = acc[(z + k) % BANDS].reshape(2, 16, 1024).astype(BF)
         z_copy(k).start()
     total = acc[z].reshape(2, 16, 1024)
     for k in (3, 2, 1):

time: 39.7 us -> 39.8 us (level)
  no operation moved by 1% of the time
where the time goes in v9:
time: 39.8 us; the launch traced here: 39.5 us
  Pallas kernels  38.1 us (96%)
  local copies, waits for them, and re-layouts  0.66 us (2%)
  between operations  0.66 us (2%)
    pallas_call x1, Pallas kernels, per_device(): pl.pallas_call(kernel, out_shape=pltpu.VMEM((2, 16, 1024), F32), in_specs...  38.1 us

profile of v9, /device:TPU:0, one launch (start us, length us, event | category | flops | bytes accessed | tf_op | source)
XLA Modules:
  0.0 39.5 jit_solution(15165101916936190054)
XLA Ops:
  0.7 38.1 %shard_map.64 = f32[2,16,1024]{2,1,0:T(8,128)S(1)} custom-call(s32[1]{0:T(128)S(6)} %copy.9.counts, s32[2,8]{1,0:T(2,128)} %bitcast.5, bf16[2,128,256]{2,1,0:T(8,128)(2,1)} %probe.1, f32[2,4,256,1024]{3,2,1,0:T(8,128)} %bitcast.4, f32[8,128,256]{2,1,0:T(8,128)} %measured.1, bf16[4,512,512]{2,1,0:T(8,128)(2,1)} %constant.2.clone.tabs_in), custom_call_target="tpu_custom_call" | custom-call | flops 4294967296 | bytes 12582912 | tf_op jit(solution)/shard_map/pallas_call | solution.py:382
  38.8 0.7 %copy.8 = f32[1,2,16,1024]{3,2,1,0:T(8,128)} copy(f32[1,2,16,1024]{3,2,1,0:T(8,128)S(1)} %bitcast.3) | data formatting | bytes 262144

commit v10 on v9

--- a/solution.py
+++ b/solution.py
@@ -286,11 +286,11 @@
     desc_a = descent(far_field(0, wave_a))
     put(0, 1, wave_a, desc_a)
     send_pieces(0, 1)
-    wave_b = first_wave(1)
     desc_a = first_descent(0, desc_a)
     put(0, 0, load(rolled, 0), desc_a)
     send_pieces(0, 0)
     send_here(0)
+    wave_b = first_wave(1)
     desc_b = descent(far_field(1, wave_b))
     put(1, 1, wave_b, desc_b)
     send_pieces(1, 1)

time: 39.8 us -> 39 us (0.980)
  Pallas kernels: 38.1 us -> 37.3 us
    pallas_call x1, Pallas kernels: 38.1 us -> 37.3 us  [per_device(): pl.pallas_call(kernel, out_shape=pltpu.VMEM((2, 16, 1024), F32), in_specs...]
where the time goes in v10:
time: 39 us; the launch traced here: 38.7 us
  Pallas kernels  37.3 us (96%)
  local copies, waits for them, and re-layouts  0.66 us (2%)
  between operations  0.66 us (2%)
    pallas_call x1, Pallas kernels, per_device(): pl.pallas_call(kernel, out_shape=pltpu.VMEM((2, 16, 1024), F32), in_specs...  37.3 us

profile of v10, /device:TPU:0, one launch (start us, length us, event | category | flops | bytes accessed | tf_op | source)
XLA Modules:
  0.0 38.7 jit_solution(5572409713784750190)
XLA Ops:
  0.7 37.3 %shard_map.64 = f32[2,16,1024]{2,1,0:T(8,128)S(1)} custom-call(s32[1]{0:T(128)S(6)} %copy.9.counts, s32[2,8]{1,0:T(2,128)} %bitcast.5, bf16[2,128,256]{2,1,0:T(8,128)(2,1)} %probe.1, f32[2,4,256,1024]{3,2,1,0:T(8,128)} %bitcast.4, f32[8,128,256]{2,1,0:T(8,128)} %measured.1, bf16[4,512,512]{2,1,0:T(8,128)(2,1)} %constant.2.clone.tabs_in), custom_call_target="tpu_custom_call" | custom-call | flops 4294967296 | bytes 12582912 | tf_op jit(solution)/shard_map/pallas_call | solution.py:382
  38.0 0.7 %copy.8 = f32[1,2,16,1024]{3,2,1,0:T(8,128)} copy(f32[1,2,16,1024]{3,2,1,0:T(8,128)S(1)} %bitcast.3) | data formatting | bytes 262144

commit v11 on v10

--- a/solution.py
+++ b/solution.py
@@ -187,8 +187,6 @@
     send_part(0, 0)
     offs_copy.wait_recv()
     send_part(0, 1)
-    send_part(1, 0)
-    send_part(1, 1)
 
     def window(s, i):
         return [t_all[s, i, p].astype(F32) for p in range(2)]
@@ -212,6 +210,8 @@
     probe_copy.wait_recv()
     meas_copy.wait_recv()
     prepare(0)
+    send_part(1, 0)
+    send_part(1, 1)
     for k in range(1, PLANE):
         place_copy(k).start()
     load_tabs.wait()

time: 39 us -> 39 us (level)
  no operation moved by 1% of the time
where the time goes in v11:
time: 39 us; the launch traced here: 38.7 us
  Pallas kernels  37.3 us (96%)
  local copies, waits for them, and re-layouts  0.66 us (2%)
  between operations  0.66 us (2%)
    pallas_call x1, Pallas kernels, per_device(): pl.pallas_call(kernel, out_shape=pltpu.VMEM((2, 16, 1024), F32), in_specs...  37.3 us

profile of v11, /device:TPU:0, one launch (start us, length us, event | category | flops | bytes accessed | tf_op | source)
XLA Modules:
  0.0 38.7 jit_solution(16589818641987405662)
XLA Ops:
  0.7 37.3 %shard_map.64 = f32[2,16,1024]{2,1,0:T(8,128)S(1)} custom-call(s32[1]{0:T(128)S(6)} %copy.9.counts, s32[2,8]{1,0:T(2,128)} %bitcast.5, bf16[2,128,256]{2,1,0:T(8,128)(2,1)} %probe.1, f32[2,4,256,1024]{3,2,1,0:T(8,128)} %bitcast.4, f32[8,128,256]{2,1,0:T(8,128)} %measured.1, bf16[4,512,512]{2,1,0:T(8,128)(2,1)} %constant.2.clone.tabs_in), custom_call_target="tpu_custom_call" | custom-call | flops 4294967296 | bytes 12582912 | tf_op jit(solution)/shard_map/pallas_call | solution.py:382
  38.0 0.7 %copy.8 = f32[1,2,16,1024]{3,2,1,0:T(8,128)} copy(f32[1,2,16,1024]{3,2,1,0:T(8,128)S(1)} %bitcast.3) | data formatting | bytes 262144
